TPU v7x, 256 devices: a whole 4x4x8 slice. The times are simulated.
256 devices in a mesh: expert: 8 (over z), vocab: 8 (over x, core), batch: 4 (over y).
Axes of the slice: x: 4, y: 4, z: 8, core: 2. Of those that a mesh axis runs over, the one named last changes fastest.
Arguments:
- resid: bfloat16 [4, 512, 6144], P('batch', ('expert', 'vocab')), may hold values from -6 to 6
- moe_gain: float32 [6144], replicated, may hold values from 0.25 to 2.5
- final_gain: float32 [6144], replicated, may hold values from 0.5 to 1.5
- router: bfloat16 [6144, 8], replicated, may hold values from -0.078125 to 0.078125
- w_gate: bfloat16 [8, 6144, 8192], P('expert', None, ('vocab', 'batch')), may hold values from -0.078125 to 0.078125
- w_up: bfloat16 [8, 6144, 8192], P('expert', None, ('vocab', 'batch')), may hold values from -0.078125 to 0.078125
- w_down: bfloat16 [8, 8192, 6144], P('expert', ('vocab', 'batch')), may hold values from -0.0625 to 0.0625
- lm_head: bfloat16 [16384, 6144], P(('expert', 'vocab')), may hold values from -6 to 6
- expert_ids: int32 [4, 512, 2], P('batch', ('expert', 'vocab')), may hold values from 0 to 7, all different within a row; in each aligned block of 8 rows (0 to 7, 8 to 15, ..., all dimensions but the last counted through in order) at most 3 rows name the same one
- target_ids: int32 [4, 512], P('batch'), may hold values from 0 to 16383
- choice_len: int32 [4, 16], P('batch'), may hold values from 1 to 64, 512 in all within a row
- choice_question: int32 [4, 16], P('batch'), may hold values from 0 to 3, as said below
Outputs:
- token_logprob: float32 [4, 512], P('batch', ('expert', 'vocab'))
- choice_prob: float32 [4, 16], P('batch')
Inputs may be any that keep to these rules, and one draw needn't show every extreme that they name: `expert_ids`: A token's 2 experts differ; the rows of one device name each expert at most 3 times. `choice_len`: each group's lengths sum to 512. `choice_question`: in each group every question number appears exactly four times.
All inputs are finite; a program needn't handle non-finite values.
Results may differ from a plain program's by a relative error of at most 0.019.
Values may be sent and summed in bfloat16 or wider, within the bound.
No kernel may reach another device: no remote copies, remote signals or barrier semaphores. Data moves between devices by JAX's collectives and lax.ppermute only.
A program may use at most 128 MiB of HBM per device.

v0:
```python
import jax
import jax.numpy as jnp
from jax import lax
from jax.sharding import PartitionSpec as P

epsilon = 1e-05


def copy_for_each(array, axis):
    peers = lax.axis_size(axis)
    return lax.all_to_all(
        jnp.broadcast_to(array[None], (peers, *array.shape)), axis, 0, 0, tiled=True
    )


def gathered_once(array, axis):
    leaves = jax.tree.leaves(array)
    order = sorted(range(len(leaves)), key=lambda k: -leaves[k].size)
    width = (1, *leaves[order[0]].shape)[-1]
    lines = [
        jnp.pad(leaves[k].reshape(-1), (0, -leaves[k].size % width)).reshape(-1, width)
        for k in order
    ]
    both, at, found = (copy_for_each(jnp.concatenate(lines), axis), 0, {})
    for k, line in zip(order, lines):
        slab = both[:, at : at + len(line)].reshape(len(both), -1)
        found[k] = slab[:, : leaves[k].size].reshape(-1, *leaves[k].shape)
        at += len(line)
    numbers = iter(range(len(leaves)))
    return jax.tree.map(lambda _: found[next(numbers)], array)


def joined_by_halves(pieces, combine):
    while len(jax.tree.leaves(pieces)[0]) > 1:
        pieces = jax.vmap(combine)(
            *(jax.tree.map(lambda part: part[side::2], pieces) for side in (0, 1))
        )
    return jax.tree.map(lambda part: part[0], pieces)


def joined_all(array, axis, combine):
    pieces = gathered_once(array, axis)
    return joined_by_halves(pieces, combine)


def rms_scale(values, gain):
    mean_square = jnp.mean(values * values, axis=-1, keepdims=True)
    return values * lax.rsqrt(mean_square + epsilon) * gain


def route_gates(router_logit, route_ids):
    expert_count = router_logit.shape[1]
    matches = route_ids[:, :, None] == jnp.arange(expert_count, dtype=jnp.int32)[None, None, :]
    picked = jnp.sum(jnp.where(matches, router_logit[:, None, :], 0.0), axis=2)
    return 1.0 / jnp.sum(jnp.exp(picked[:, None, :] - picked[:, :, None]), axis=2)


def expand_rows(block_rows, gate_cols, up_cols):
    gate_part = jnp.dot(block_rows, gate_cols, preferred_element_type=jnp.float32)
    up_part = jnp.dot(block_rows, up_cols, preferred_element_type=jnp.float32)
    return (jax.nn.silu(gate_part) * up_part).astype(jnp.bfloat16)


def choice_member(lengths, positions):
    ends = jnp.cumsum(lengths, dtype=jnp.int32)
    starts = ends - lengths
    return (positions[None, :] >= starts[:, None]) & (positions[None, :] < ends[:, None])


def choice_softmax(choice_total, lengths, questions):
    average = choice_total / lengths.astype(jnp.float32)
    same_question = questions[:, None] == questions[None, :]
    question_top = jnp.max(jnp.where(same_question, average[None, :], -jnp.inf), axis=1)
    raised = jnp.exp(average - question_top)
    denominator = jnp.sum(jnp.where(same_question, raised[None, :], 0.0), axis=1)
    return raised / denominator


def merge_stats(first, second):
    top_value = jnp.maximum(first[0], second[0])
    summed = first[1] * jnp.exp(first[0] - top_value) + second[1] * jnp.exp(second[0] - top_value)
    return (top_value, summed, first[2] + second[2])


def on_device(
    resid,
    moe_gain,
    final_gain,
    router,
    w_gate,
    w_up,
    w_down,
    lm_head,
    expert_ids,
    target_ids,
    choice_len,
    choice_question,
):
    stream = resid[0].astype(jnp.float32)
    token_count, model_width = stream.shape
    normed_in = rms_scale(stream, moe_gain).astype(jnp.bfloat16)
    router_logit = jnp.dot(normed_in, router, preferred_element_type=jnp.float32)
    route_ids = expert_ids[0]
    route_count = route_ids.shape[1]
    gate_weights = route_gates(router_logit, route_ids)
    expert_count = lax.axis_size("expert")
    bucket_size = max(2, (token_count * route_count + expert_count - 1) // expert_count + 1)
    flat_ids = route_ids.reshape(-1)
    expert_match = (flat_ids[:, None] == jnp.arange(expert_count, dtype=jnp.int32)[None, :]).astype(
        jnp.int32
    )
    earlier = jnp.cumsum(expert_match, axis=0, dtype=jnp.int32) - expert_match
    slot_index = flat_ids * bucket_size + jnp.sum(earlier * expert_match, axis=1)
    slot_match = (
        slot_index[:, None] == jnp.arange(expert_count * bucket_size, dtype=jnp.int32)[None, :]
    ).astype(jnp.float32)
    slot_match = slot_match.reshape(token_count, route_count, -1)
    dispatch = jnp.sum(slot_match, axis=1).astype(jnp.bfloat16)
    combine_weights = jnp.sum(slot_match * gate_weights[:, :, None], axis=1)
    buckets = lax.dot_general(
        dispatch, normed_in, (((0,), (0,)), ((), ())), preferred_element_type=jnp.float32
    )
    buckets = buckets.astype(jnp.bfloat16).reshape(expert_count, bucket_size, model_width)
    gate_cols = w_gate[0]
    up_cols = w_up[0]
    down_rows = w_down[0]
    arrived = lax.all_to_all(buckets, "expert", split_axis=0, concat_axis=0, tiled=True).reshape(
        -1, model_width
    )
    hidden = expand_rows(
        lax.all_gather(arrived, ("vocab", "batch"), axis=0, tiled=True), gate_cols, up_cols
    )
    expert_sum = lax.psum_scatter(
        jnp.dot(hidden, down_rows, preferred_element_type=jnp.float32).astype(jnp.bfloat16),
        ("vocab", "batch"),
        scatter_dimension=0,
        tiled=True,
    )
    outgoing = expert_sum.reshape(expert_count, bucket_size, model_width)
    returned = lax.all_to_all(outgoing, "expert", split_axis=0, concat_axis=0, tiled=True)
    returned_rows = returned.reshape(-1, model_width).astype(jnp.float32)
    mixed_rows = stream + jnp.dot(combine_weights, returned_rows)
    normed_out = rms_scale(mixed_rows, final_gain).astype(jnp.bfloat16)
    head_index = lax.axis_index(("expert", "vocab"))
    vocab_share = lm_head.shape[0]
    vocab_ids = jnp.arange(vocab_share, dtype=jnp.int32) + head_index * vocab_share
    targets = target_ids[0]
    group_tokens = targets.shape[0]
    logits = lax.dot_general(
        lax.all_gather(normed_out, ("expert", "vocab"), axis=0, tiled=True),
        lm_head,
        (((1,), (1,)), ((), ())),
        preferred_element_type=jnp.float32,
    )
    block_top = jnp.max(logits, axis=1)
    block_sum = jnp.sum(jnp.exp(logits - block_top[:, None]), axis=1)
    block_hit = jnp.sum(jnp.where(targets[:, None] == vocab_ids[None, :], logits, 0.0), axis=1)
    fresh = (block_top, block_sum, block_hit)
    largest, spread_sum, chosen = tuple((fresh[slot] for slot in range(3)))
    lengths = choice_len[0]
    questions = choice_question[0]
    own_first = head_index * token_count
    group_positions = jnp.arange(group_tokens, dtype=jnp.int32)
    best, summed, target_sum = joined_all(
        (largest, spread_sum, chosen), ("expert", "vocab"), merge_stats
    )
    group_logprob = target_sum - (best + jnp.log(summed))
    choice_total = jnp.sum(
        jnp.where(choice_member(lengths, group_positions), group_logprob[None, :], 0.0), axis=1
    )
    own_logprob = lax.dynamic_slice_in_dim(group_logprob, own_first, token_count, 0)
    choice_prob = choice_softmax(choice_total, lengths, questions)
    return (own_logprob.reshape(1, -1), choice_prob.reshape(1, -1))


def solution(mesh):
    return jax.shard_map(
        on_device,
        mesh=mesh,
        in_specs=(
            P("batch", ("expert", "vocab"), None),
            P(),
            P(),
            P(),
            P("expert", None, ("vocab", "batch")),
            P("expert", None, ("vocab", "batch")),
            P("expert", ("vocab", "batch"), None),
            P(("expert", "vocab"), None),
            P("batch", ("expert", "vocab"), None),
            P("batch", None),
            P("batch", None),
            P("batch", None),
        ),
        out_specs=(P("batch", ("expert", "vocab")), P("batch", None)),
        check_vma=False,
    )
```

profile of v0, /device:TPU:1, one launch (start us, length us, event | category | flops | bytes accessed | tf_op | source)
XLA Modules:
  0.0 376.1 jit_solution(1491115489635027238)
XLA Ops:
  7.2 0.9 copy.31
  8.1 0.1 eq.72
  8.2 0.1 fusion.28
  8.3 0.2 select_reduce_fusion.4
  8.5 0.1 reduce_sum.106
  8.6 0.1 copy.32
  8.7 0.7 multiply_add_fusion.5
  9.4 1.1 fusion.19
  10.4 1.2 fusion.24
  11.6 0.8 select_reduce_fusion.3
  12.5 0.1 convert_reduce_fusion
  12.6 1.9 convolution_convert_fusion.1
  14.5 1.1 reshape.128
  15.6 22.4 %all_to_all.15 = bf16[8,3,6144]{2,1,0:T(4,128)(2,1)} all-to-all(bf16[8,3,6144]{2,1,0:T(4,128)(2,1)S(1)} %reshape.128), channel_id=1, replica_groups=mesh['expert'=8,'vocab'=8,'batch'=4] {'expert'}, dimensions={0} | all-to-all | bytes 589824 | tf_op jit(solution)/shard_map/all_to_all | solution.py:127
  38.1 2.0 reshape.129
  40.0 0.0 reduce-scatter.2.cloned.1.call-start
  40.1 58.8 %all-gather.3.cloned.1.call-done = bf16[768,6144]{1,0:T(8,128)(2,1)} async-done(((bf16[24,6144]{1,0:T(8,128)(2,1)}), bf16[768,6144]{1,0:T(8,128)(2,1)}) %all-gather.3.cloned.1.call-update) | async-done | bytes 9437200 | tf_op jit(solution)/shard_map/all_gather | solution.py:131
  98.9 8.1 %fusion.3 = f32[768,256]{1,0:T(8,128)} fusion(bf16[768,6144]{1,0:T(8,128)(2,1)} %all-gather.3.cloned.1.call-done, bf16[1,6144,256]{2,1,0:T(8,128)(2,1)} %param.16), kind=kOutput, calls=%fused_computation.6 | convolution fusion | flops 2415919104 | bytes 13369344 | tf_op jit(solution)/shard_map/dot_general | solution.py:59
  106.9 19.4 %convolution_convert_fusion = bf16[768,6144]{1,0:T(8,128)(2,1)} fusion(bf16[1,256,6144]{2,1,0:T(8,128)(2,1)S(1)} %copy-done, bf16[768,6144]{1,0:T(8,128)(2,1)} %all-gather.3.cloned.1.call-done, bf16[1,6144,256]{2,1,0:T(8,128)(2,1)} %param.17, f32[768,256]{1,0:T(8,128)} %fusion.3), kind=kOutput, calls=%fused_computation | convolution fusion | flops 4837736448 | bytes 25952256 | tf_op jit(solution)/shard_map/dot_general | solution.py:134
  126.3 0.0 all-gather.5.cloned.1.call-start
  126.4 100.8 %reduce-scatter.2.cloned.1.call-done = bf16[24,6144]{1,0:T(8,128)(2,1)} async-done(((bf16[768,6144]{1,0:T(8,128)(2,1)}), bf16[24,6144]{1,0:T(8,128)(2,1)}) %reduce-scatter.2.cloned.1.call-update) | async-done | bytes 294928 | tf_op jit(solution)/shard_map/reduce_scatter | solution.py:133
  227.2 1.1 reshape.130
  228.4 18.1 %all_to_all.16 = bf16[8,3,6144]{2,1,0:T(4,128)(2,1)} all-to-all(bf16[8,3,6144]{2,1,0:T(4,128)(2,1)S(1)} %reshape.130), channel_id=1, replica_groups=mesh['expert'=8,'vocab'=8,'batch'=4] {'expert'}, dimensions={0} | all-to-all | bytes 589824 | tf_op jit(solution)/shard_map/all_to_all | solution.py:140
  246.5 1.2 reshape.131
  247.7 1.2 multiply_reduce_fusion
  248.9 1.5 multiply_convert_fusion
  250.5 79.1 %all-gather.5.cloned.1.call-done = bf16[512,6144]{1,0:T(8,128)(2,1)} async-done(((bf16[8,6144]{1,0:T(8,128)(2,1)}), bf16[512,6144]{1,0:T(8,128)(2,1)}) %all-gather.5.cloned.1.call-update) | async-done | bytes 6291472 | tf_op jit(solution)/shard_map/all_gather | solution.py:150
  329.6 5.5 %fusion.37 = (f32[512]{0:T(512)S(1)}, f32[512,256]{0,1:T(8,128)S(1)}) fusion(bf16[512,6144]{1,0:T(8,128)(2,1)} %all-gather.5.cloned.1.call-done, bf16[256,6144]{1,0:T(8,128)(2,1)} %param.19), kind=kOutput, calls=%fused_computation.74 | convolution fusion | flops 1610743296 | bytes 9963520 | tf_op jit(solution)/shard_map/dot_general | solution.py:149
  335.2 0.1 exponential_reduce_fusion
  335.3 0.9 broadcast_in_dim.84
  336.2 5.9 %all-to-all-start.2 = ((f32[64,3,512]{2,1,0:T(4,128)}), f32[64,3,512]{2,1,0:T(4,128)}, u32[]{:S(2)}, u32[]{:S(2)}) async-start(f32[64,3,512]{2,1,0:T(4,128)} %broadcast_in_dim.84), calls=%async_computation.3 | async-start | bytes 1048576 | tf_op jit(solution)/shard_map/all_to_all | solution.py:11
  342.1 0.1 copy.35
  342.2 0.1 reduce
  342.3 0.5 bitcast_subtract_fusion.1
  342.8 16.9 %all-to-all-done.2 = f32[64,3,512]{2,1,0:T(4,128)} async-done(((f32[64,3,512]{2,1,0:T(4,128)}), f32[64,3,512]{2,1,0:T(4,128)}, u32[]{:S(2)}, u32[]{:S(2)}) %all-to-all-start.2) | async-done | bytes 393248 | tf_op jit(solution)/shard_map/all_to_all | solution.py:11
  359.7 1.8 fusion.36
  361.5 0.6 slice.124
  362.1 0.6 slice.125
  362.8 0.9 add.97
  363.9 0.6 slice.138
  364.6 0.6 slice.137
  365.2 0.9 multiply_add_fusion
  366.6 0.6 constant_dynamic-slice_fusion
  367.2 0.8 select_reduce_fusion.1
  368.0 0.7 bitcast_divide_fusion.1
  368.7 0.2 fusion.26
  368.9 0.2 fusion.27
  369.1 0.5 bitcast_divide_fusion
  (58 shorter events, 1.0 us)
Async XLA Ops:
  7.2 99.8 %copy-start = (bf16[1,256,6144]{2,1,0:T(8,128)(2,1)S(1)}, bf16[1,256,6144]{2,1,0:T(8,128)(2,1)}, u32[]{:S(2)}) copy-start(bf16[1,256,6144]{2,1,0:T(8,128)(2,1)} %param.18) | copy-start | bytes 9437188
  7.2 91.7 %all-gather.3.cloned.1.call-start = ((), (), s32[]{:S(2)}) async-start(), calls=%async_computation.4 | async-start | bytes 9732096 | tf_op jit(solution)/shard_map/all_gather | solution.py:131
  40.0 187.2 %reduce-scatter.2.cloned.1.call-start = ((), (), s32[]{:S(2)}) async-start(), calls=%async_computation.5 | async-start | bytes 9732096 | tf_op jit(solution)/shard_map/reduce_scatter | solution.py:133
  126.3 203.3 %all-gather.5.cloned.1.call-start = ((), (), s32[]{:S(2)}) async-start(), calls=%async_computation.6 | async-start | bytes 6389760 | tf_op jit(solution)/shard_map/all_gather | solution.py:150
  250.4 84.7 %copy-start.2 = (s32[1,512]{1,0:T(1,128)S(1)}, s32[1,512]{1,0:T(1,128)}, u32[]{:S(2)}) copy-start(s32[1,512]{1,0:T(1,128)} %param.21) | copy-start | bytes 6148
  250.5 91.6 %copy-start.3 = (s32[1,16]{1,0:T(1,128)S(1)}, s32[1,16]{1,0:T(1,128)}, u32[]{:S(2)}) copy-start(s32[1,16]{1,0:T(1,128)} %param.22) | copy-start | bytes 196
  335.2 33.5 %copy-start.1 = (s32[1,16]{1,0:T(1,128)S(1)}, s32[1,16]{1,0:T(1,128)}, u32[]{:S(2)}) copy-start(s32[1,16]{1,0:T(1,128)} %param.23) | copy-start | bytes 196
  336.2 23.5 %all-to-all-start.2 = ((f32[64,3,512]{2,1,0:T(4,128)}), f32[64,3,512]{2,1,0:T(4,128)}, u32[]{:S(2)}, u32[]{:S(2)}) async-start(f32[64,3,512]{2,1,0:T(4,128)} %broadcast_in_dim.84), calls=%async_computation.3 | async-start | bytes 1048576 | tf_op jit(solution)/shard_map/all_to_all | solution.py:11
Sparse Core Ops, SparseCore 0:
  40.2 58.6 all-gather.2
  126.5 100.7 reduce-scatter.1
  250.5 79.0 all-gather.4
where the time goes:
time: 377 us; the launch traced here: 376 us
  waiting for transfers between devices  256 us (68%)
  blocking collectives  40.6 us (11%)
  matrix products  37.3 us (10%)
  between operations  14 us (4%)
  local copies, waits for them, and re-layouts  13.1 us (3%)
  other arithmetic  9.63 us (3%)
  starting transfers between devices  5.98 us (2%)
    reduce_scatter x1, waiting for transfers between devices, on_device(): lax.psum_scatter(jnp.dot(hidden, down_rows, preferred_element_type=jnp.fl...  101 us
    all_gather x1, waiting for transfers between devices, on_device(): lax.all_gather(normed_out, ('expert', 'vocab'), axis=0, tiled=True)  79.1 us
    all_gather x1, waiting for transfers between devices, on_device(): lax.all_gather(arrived, ('vocab', 'batch'), axis=0, tiled=True)  58.8 us
    all_to_all x1, blocking collectives, on_device(): lax.all_to_all(buckets, 'expert', split_axis=0, concat_axis=0, tiled=True)  22.4 us
    dot_general x1, matrix products, on_device(): jnp.dot(hidden, down_rows, preferred_element_type=jnp.float32)  19.4 us
    all_to_all x1, blocking collectives, on_device(): lax.all_to_all(outgoing, 'expert', split_axis=0, concat_axis=0, tiled=True)  18.1 us
    all_to_all x1, waiting for transfers between devices, copy_for_each(): lax.all_to_all(jnp.broadcast_to(array[None], (peers, *array.shape)), axis...  16.9 us
    dot_general x1, matrix products, expand_rows(): jnp.dot(block_rows, gate_cols, preferred_element_type=jnp.float32)  8.09 us
  transfers between devices with their start and end apart: 4, of which 4 were waited for; matrix products, arithmetic and copies ran while one was open for 0% of the time, Pallas kernels for 0%

commit v1 on v0

--- a/solution.py
+++ b/solution.py
@@ -128,7 +128,14 @@
         -1, model_width
     )
     hidden = expand_rows(
-        lax.all_gather(arrived, ("vocab", "batch"), axis=0, tiled=True), gate_cols, up_cols
+        jnp.concatenate(
+            lax.all_to_all(
+                jnp.stack([arrived] * lax.axis_size(("vocab", "batch"))), ("vocab", "batch"), 0, 0
+            ),
+            axis=0,
+        ),
+        gate_cols,
+        up_cols,
     )
     expert_sum = lax.psum_scatter(
         jnp.dot(hidden, down_rows, preferred_element_type=jnp.float32).astype(jnp.bfloat16),

time: 377 us -> 428 us (1.14)
  blocking collectives: 40.6 us -> 156 us
  waiting for transfers between devices: 256 us -> 191 us
  matrix products: 37.3 us -> 32.7 us
    all_to_all x0 -> x1, blocking collectives: none -> 115 us  [on_device(): lax.all_to_all(jnp.stack([arrived] * lax.axis_size(('vocab', 'batch'))),...]
    all_gather x1 -> x0, waiting for transfers between devices: 58.8 us -> none  [on_device(): lax.all_gather(arrived, ('vocab', 'batch'), axis=0, tiled=True)]
    reduce_scatter x1, waiting for transfers between devices: 101 us -> 95.2 us  [on_device(): lax.psum_scatter(jnp.dot(hidden, down_rows, preferred_element_type=jnp.fl...]
    dot_general x1, matrix products: 8.09 us -> 3.55 us  [expand_rows(): jnp.dot(block_rows, gate_cols, preferred_element_type=jnp.float32)]
  transfers between devices with their start and end apart: 4 -> 3, of which waited for: 4 -> 3; matrix products, arithmetic and copies ran while one was open for 0% -> 0% of each run, Pallas kernels for 0% -> 0%
where the time goes in v1:
time: 428 us; the launch traced here: 427 us
  waiting for transfers between devices  191 us (45%)
  blocking collectives  156 us (36%)
  matrix products  32.7 us (8%)
  local copies, waits for them, and re-layouts  17.2 us (4%)
  between operations  14.3 us (3%)
  other arithmetic  9.63 us (2%)
  starting transfers between devices  5.92 us (1%)
    all_to_all x1, blocking collectives, on_device(): lax.all_to_all(jnp.stack([arrived] * lax.axis_size(('vocab', 'batch'))),...  115 us
    reduce_scatter x1, waiting for transfers between devices, on_device(): lax.psum_scatter(jnp.dot(hidden, down_rows, preferred_element_type=jnp.fl...  95.2 us
    all_gather x1, waiting for transfers between devices, on_device(): lax.all_gather(normed_out, ('expert', 'vocab'), axis=0, tiled=True)  79.2 us
    all_to_all x1, blocking collectives, on_device(): lax.all_to_all(buckets, 'expert', split_axis=0, concat_axis=0, tiled=True)  22.4 us
    dot_general x1, matrix products, on_device(): jnp.dot(hidden, down_rows, preferred_element_type=jnp.float32)  19.4 us
    all_to_all x1, blocking collectives, on_device(): lax.all_to_all(outgoing, 'expert', split_axis=0, concat_axis=0, tiled=True)  18.1 us
    all_to_all x1, waiting for transfers between devices, copy_for_each(): lax.all_to_all(jnp.broadcast_to(array[None], (peers, *array.shape)), axis...  16.9 us
  transfers between devices with their start and end apart: 3, of which 3 were waited for; matrix products, arithmetic and copies ran while one was open for 0% of the time, Pallas kernels for 0%

profile of v1, /device:TPU:1, one launch (start us, length us, event | category | flops | bytes accessed | tf_op | source)
XLA Modules:
  0.0 427.0 jit_solution(11019909115493849214)
XLA Ops:
  7.2 0.9 copy.31
  8.1 0.1 eq.72
  8.2 0.1 fusion.28
  8.3 0.2 select_reduce_fusion.4
  8.5 0.1 reduce_sum.106
  8.6 0.1 copy.32
  8.7 0.7 multiply_add_fusion.5
  9.4 1.1 fusion.19
  10.4 1.2 fusion.24
  11.6 0.8 select_reduce_fusion.3
  12.5 0.1 convert_reduce_fusion
  12.6 1.9 convolution_convert_fusion.1
  14.5 1.1 reshape.130
  15.6 22.4 %all_to_all.20 = bf16[8,3,6144]{2,1,0:T(4,128)(2,1)} all-to-all(bf16[8,3,6144]{2,1,0:T(4,128)(2,1)S(1)} %reshape.130), channel_id=1, replica_groups=mesh['expert'=8,'vocab'=8,'batch'=4] {'expert'}, dimensions={0} | all-to-all | bytes 589824 | tf_op jit(solution)/shard_map/all_to_all | solution.py:127
  38.0 1.2 stack_reshape.2
  39.3 1.2 stack.3
  40.5 115.4 %all_to_all.21 = bf16[32,24,6144]{2,1,0:T(8,128)(2,1)S(1)} all-to-all(bf16[32,24,6144]{2,1,0:T(8,128)(2,1)S(1)} %stack.3), channel_id=1, replica_groups=mesh['expert'=8,'vocab'=8,'batch'=4] {'vocab','batch'}, dimensions={0} | all-to-all | bytes 18874368 | tf_op jit(solution)/shard_map/all_to_all | solution.py:132
  155.9 3.7 copy-done.1
  159.5 3.5 fusion.3
  163.1 19.4 %convolution_convert_fusion = bf16[768,6144]{1,0:T(8,128)(2,1)} fusion(bf16[1,256,6144]{2,1,0:T(8,128)(2,1)S(1)} %copy-done, bf16[768,6144]{1,0:T(8,128)(2,1)} %bitcast.65, bf16[1,6144,256]{2,1,0:T(8,128)(2,1)} %param.17, f32[768,256]{1,0:T(8,128)} %fusion.3), kind=kOutput, calls=%fused_computation | convolution fusion | flops 4837736448 | bytes 25952256 | tf_op jit(solution)/shard_map/dot_general | solution.py:141
  182.5 95.2 %reduce-scatter.2.cloned.1.call-done = bf16[24,6144]{1,0:T(8,128)(2,1)} async-done(((bf16[768,6144]{1,0:T(8,128)(2,1)}), bf16[24,6144]{1,0:T(8,128)(2,1)}) %reduce-scatter.2.cloned.1.call-update) | async-done | bytes 294928 | tf_op jit(solution)/shard_map/reduce_scatter | solution.py:140
  277.8 1.1 reshape.132
  278.9 18.1 %all_to_all.22 = bf16[8,3,6144]{2,1,0:T(4,128)(2,1)} all-to-all(bf16[8,3,6144]{2,1,0:T(4,128)(2,1)S(1)} %reshape.132), channel_id=1, replica_groups=mesh['expert'=8,'vocab'=8,'batch'=4] {'expert'}, dimensions={0} | all-to-all | bytes 589824 | tf_op jit(solution)/shard_map/all_to_all | solution.py:147
  297.0 1.2 reshape.133
  298.2 1.2 multiply_reduce_fusion
  299.4 1.5 multiply_convert_fusion
  301.0 79.2 %all-gather.2.cloned.1.call-done = bf16[512,6144]{1,0:T(8,128)(2,1)} async-done(((bf16[8,6144]{1,0:T(8,128)(2,1)}), bf16[512,6144]{1,0:T(8,128)(2,1)}) %all-gather.2.cloned.1.call-update) | async-done | bytes 6291472 | tf_op jit(solution)/shard_map/all_gather | solution.py:157
  380.2 5.5 %fusion.37 = (f32[512]{0:T(512)S(1)}, f32[512,256]{0,1:T(8,128)S(1)}) fusion(bf16[512,6144]{1,0:T(8,128)(2,1)} %all-gather.2.cloned.1.call-done, bf16[256,6144]{1,0:T(8,128)(2,1)} %param.19), kind=kOutput, calls=%fused_computation.74 | convolution fusion | flops 1610743296 | bytes 9963520 | tf_op jit(solution)/shard_map/dot_general | solution.py:156
  385.8 0.1 exponential_reduce_fusion
  385.9 0.9 broadcast_in_dim.84
  386.8 5.8 %all-to-all-start.3 = ((f32[64,3,512]{2,1,0:T(4,128)}), f32[64,3,512]{2,1,0:T(4,128)}, u32[]{:S(2)}, u32[]{:S(2)}) async-start(f32[64,3,512]{2,1,0:T(4,128)} %broadcast_in_dim.84), calls=%async_computation.4 | async-start | bytes 1048576 | tf_op jit(solution)/shard_map/all_to_all | solution.py:11
  392.7 0.1 copy.35
  392.8 0.1 reduce
  392.9 0.5 bitcast_subtract_fusion.1
  393.4 16.9 %all-to-all-done.3 = f32[64,3,512]{2,1,0:T(4,128)} async-done(((f32[64,3,512]{2,1,0:T(4,128)}), f32[64,3,512]{2,1,0:T(4,128)}, u32[]{:S(2)}, u32[]{:S(2)}) %all-to-all-start.3) | async-done | bytes 393248 | tf_op jit(solution)/shard_map/all_to_all | solution.py:11
  410.3 1.8 fusion.36
  412.1 0.6 slice.124
  412.7 0.6 slice.125
  413.4 0.9 add.97
  414.6 0.6 slice.138
  415.2 0.6 slice.137
  415.8 0.9 multiply_add_fusion
  417.2 0.6 constant_dynamic-slice_fusion
  417.8 0.8 select_reduce_fusion.1
  418.6 0.7 bitcast_divide_fusion.1
  419.3 0.2 fusion.26
  419.5 0.2 fusion.27
  419.7 0.5 bitcast_divide_fusion
  (61 shorter events, 1.0 us)
Async XLA Ops:
  7.2 155.9 %copy-start = (bf16[1,256,6144]{2,1,0:T(8,128)(2,1)S(1)}, bf16[1,256,6144]{2,1,0:T(8,128)(2,1)}, u32[]{:S(2)}) copy-start(bf16[1,256,6144]{2,1,0:T(8,128)(2,1)} %param.18) | copy-start | bytes 9437188
  7.2 270.6 %reduce-scatter.2.cloned.1.call-start = ((), (), s32[]{:S(2)}) async-start(), calls=%async_computation.5 | async-start | bytes 9732096 | tf_op jit(solution)/shard_map/reduce_scatter | solution.py:140
  40.5 119.1 %copy-start.5 = (bf16[1,6144,256]{2,1,0:T(8,128)(2,1)S(1)}, bf16[1,6144,256]{2,1,0:T(8,128)(2,1)}, u32[]{:S(2)}) copy-start(bf16[1,6144,256]{2,1,0:T(8,128)(2,1)} %param.16) | copy-start | bytes 9437188
  155.9 3.7 copy-start.1
  182.5 197.7 %all-gather.2.cloned.1.call-start = ((), (), s32[]{:S(2)}) async-start(), calls=%async_computation.6 | async-start | bytes 6389760 | tf_op jit(solution)/shard_map/all_gather | solution.py:157
  300.9 84.8 %copy-start.3 = (s32[1,512]{1,0:T(1,128)S(1)}, s32[1,512]{1,0:T(1,128)}, u32[]{:S(2)}) copy-start(s32[1,512]{1,0:T(1,128)} %param.21) | copy-start | bytes 6148
  300.9 91.7 %copy-start.4 = (s32[1,16]{1,0:T(1,128)S(1)}, s32[1,16]{1,0:T(1,128)}, u32[]{:S(2)}) copy-start(s32[1,16]{1,0:T(1,128)} %param.22) | copy-start | bytes 196
  385.8 33.5 %copy-start.2 = (s32[1,16]{1,0:T(1,128)S(1)}, s32[1,16]{1,0:T(1,128)}, u32[]{:S(2)}) copy-start(s32[1,16]{1,0:T(1,128)} %param.23) | copy-start | bytes 196
  386.8 23.5 %all-to-all-start.3 = ((f32[64,3,512]{2,1,0:T(4,128)}), f32[64,3,512]{2,1,0:T(4,128)}, u32[]{:S(2)}, u32[]{:S(2)}) async-start(f32[64,3,512]{2,1,0:T(4,128)} %broadcast_in_dim.84), calls=%async_computation.4 | async-start | bytes 1048576 | tf_op jit(solution)/shard_map/all_to_all | solution.py:11
Sparse Core Ops, SparseCore 0:
  182.6 95.1 reduce-scatter.1
  301.0 79.1 all-gather.1
